TPU v7x, 512 devices: a whole 4x8x8 slice. The times are simulated.
512 devices in a mesh: img: 32 (over y, x_hi, core), patch: 16 (over z, x_lo).
Axes of the slice: x: 4 (x_hi: 2, x_lo: 2; x = x_hi * 2 + x_lo), y: 8, z: 8, core: 2. Of those that a mesh axis runs over, the one named last changes fastest.
Arguments:
- fresh: bfloat16 [32, 16, 4, 16, 4608], P('img', 'patch'), may hold values from -9 to 9
- stale_keys: bfloat16 [32, 16, 4, 16, 1536], P('img', 'patch'), may hold values from -6 to 6
- stale_values: bfloat16 [32, 16, 4, 16, 1536], P('img', 'patch'), may hold values from -6 to 6
- text_kv: bfloat16 [32, 128, 3072], P('img'), may hold values from -6 to 6
- group_slots: int32 [32], replicated, may hold values from 1 to 3, as said below
- text_len: int32 [32], replicated, may hold values from 1 to 128, as said below
Outputs:
- attended: bfloat16 [32, 16, 4, 16, 1536], P('img', 'patch')
Inputs may be any that keep to these rules, and one draw needn't show every extreme that they name: The groups hold 2 on average; the running sums over g of group_slots[g] - 2 differ by at most 1 between any two groups. `text_len`: some group has 128.
All inputs are finite; a program needn't handle non-finite values.
Results may differ from a plain program's by a relative error of at most 0.0046.
Values may be sent and summed in bfloat16 or wider, within the bound.
A program may use at most 64 MiB of HBM per device.

v0:
```python
import functools

import jax
import jax.numpy as jnp
from jax import lax
from jax.experimental import pallas as pl
from jax.experimental.pallas import tpu as pltpu
from jax.sharding import PartitionSpec as P

MESH = pl.DeviceIdType.MESH
F32 = jnp.float32
BF16 = jnp.bfloat16

HDIM = 128
HEADS = 12
HD = HDIM * HEADS
BLK = 16
LIVE = 3
TXT = 128
PEERS = 16
IMAGES = 32
ROWS = LIVE * BLK
BLOCKS = PEERS * LIVE
TBLOCKS = TXT // BLK
KBLOCKS = BLOCKS + TBLOCKS
CHUNKS = 4
CPEERS = PEERS // CHUNKS
CBLOCKS = BLOCKS // CHUNKS
CROWS = CBLOCKS * BLK
SCALE = 1.4426950408889634 / HDIM**0.5
MASKED = -1e30


def nt(a, b):
    return lax.dot_general(a, b, (((1,), (1,)), ((), ())), preferred_element_type=F32)


def owner_rank(peer, core):
    z, x = peer // 2, peer % 2
    return lax.rem(z + 15 - 2 * core - x, 4)


def owned_head(peer, core):
    z, x = peer // 2, peer % 2
    return (z // 4) * 6 + x * 3 + owner_rank(peer, core)


def partner(me, k):
    half = k // 2
    odd = lax.rem(k, 2)
    offset = PEERS // 2 + odd * half - (1 - odd) * half
    return lax.rem(me + offset, PEERS)


def kernel(
    fresh, keys, values, text, slots_in, lengths_in, out,
    own, stale, chunks, inbox, tkeys, tvalues, qmask, kmask, pbuf, linv,
    osend, lsend, orecv, lrecv, ownout, ownlse, coef, counts,
    local_sem, text_sem, kq_sem, v_sem, o_sem, l_sem, kq_sent, v_sent, o_sent, l_sent,
):
    image = lax.axis_index("img")
    me = lax.axis_index("patch")
    core = lax.rem(image, 2)
    is_owner = owner_rank(me, core) < 3
    my_head = owned_head(me, core)

    barrier = pltpu.get_barrier_semaphore()

    def greet(k, carry):
        pl.semaphore_signal(barrier, inc=1, device_id=(image, partner(me, k)), device_id_type=MESH)
        return carry

    lax.fori_loop(1, PEERS, greet, 0)

    live = pl.ds(0, LIVE)
    local = [
        pltpu.make_async_copy(keys.at[live], stale.at[0], local_sem.at[0]),
        pltpu.make_async_copy(fresh.at[live], own, local_sem.at[1]),
        pltpu.make_async_copy(values.at[live], stale.at[1], local_sem.at[2]),
        pltpu.make_async_copy(slots_in, counts.at[0], local_sem.at[3]),
        pltpu.make_async_copy(lengths_in, counts.at[1], local_sem.at[4]),
    ]
    for copy in local:
        copy.start()

    def text_copy(third, target):
        columns = pl.ds(pl.multiple_of(third * HD + my_head * HDIM, HDIM), HDIM)
        return pltpu.make_async_copy(text.at[:, :, columns], target, text_sem.at[third])

    texts = [text_copy(0, tkeys), text_copy(1, tvalues)]

    @pl.when(is_owner)
    def _():
        for copy in texts:
            copy.start()

    def stage(part, source):
        for head in range(HEADS):
            chunks[head, part] = source[:, :, head * HDIM : (head + 1) * HDIM]

    local[0].wait()
    stage(0, stale.at[0])
    local[1].wait()
    stage(1, own)
    local[2].wait()
    stage(2, stale.at[1])

    pl.semaphore_wait(barrier, PEERS - 1)

    keys_queries = pl.ds(0, 2)
    only_values = pl.ds(2, 1)

    def send(peer, parts, sent, received):
        pltpu.make_async_remote_copy(
            src_ref=chunks.at[owned_head(peer, core), parts],
            dst_ref=inbox.at[me, parts],
            send_sem=sent,
            recv_sem=received,
            device_id=(image, peer),
            device_id_type=MESH,
        ).start()

    def send_all(parts, sent, received):
        def step(k, carry):
            peer = partner(me, k)

            @pl.when(owner_rank(peer, core) < 3)
            def _():
                send(peer, parts, sent, received)

            return carry

        lax.fori_loop(1, PEERS, step, 0)

        @pl.when(is_owner)
        def _():
            pltpu.make_async_copy(chunks.at[my_head, parts], inbox.at[me, parts], received).start()

    send_all(keys_queries, kq_sent, kq_sem)
    send_all(only_values, v_sent, v_sem)

    def wait_for(ref, sem):
        pltpu.make_async_copy(ref, ref, sem).wait()

    local[3].wait()
    local[4].wait()
    n = counts[0, image]
    length = counts[1, image]

    @pl.when(is_owner)
    def _():
        shape = (KBLOCKS, BLK, HDIM)
        block = lax.broadcasted_iota(jnp.int32, shape, 0)
        row = lax.broadcasted_iota(jnp.int32, shape, 1)
        lane = lax.broadcasted_iota(jnp.int32, shape, 2)
        slot = block - 3 * ((block * 171) >> 9)
        dead = jnp.where(block < BLOCKS, slot - n, (block - BLOCKS) * BLK + row - length) >= 0
        hit = ((lane == block) & (block < BLOCKS)) | ((lane == HDIM - 1) & dead)
        kmask[...] = jnp.where(hit, MASKED, 0.0).astype(BF16)
        shape = (BLOCKS, BLK, HDIM)
        block = lax.broadcasted_iota(jnp.int32, shape, 0)
        lane = lax.broadcasted_iota(jnp.int32, shape, 2)
        qmask[...] = jnp.where((lane == block) | (lane == HDIM - 1), 1.0, 0.0).astype(BF16)

    def attend_own(first, count):
        heads = range(first, first + count)
        diagonal = (
            lax.broadcasted_iota(jnp.int32, (ROWS, ROWS), 0) // BLK
            == lax.broadcasted_iota(jnp.int32, (ROWS, ROWS), 1) // BLK
        )

        def third(which, head):
            at = which * HD + head * HDIM
            return own[:, :, at : at + HDIM].reshape(ROWS, HDIM)

        scores = [jnp.where(diagonal, nt(third(0, head), third(1, head)), MASKED) for head in heads]
        tops = [jnp.max(x, axis=1, keepdims=True) for x in scores]
        weights = [jnp.exp2((x - top) * SCALE) for x, top in zip(scores, tops)]
        totals = [jnp.sum(x, axis=1, keepdims=True) for x in weights]
        sums = [
            jnp.dot(x.astype(BF16), third(2, head), preferred_element_type=F32) for x, head in zip(weights, heads)
        ]
        for i, head in enumerate(heads):
            ownout[head] = sums[i] / totals[i]
            ownlse[head] = jnp.broadcast_to(tops[i] * SCALE + jnp.log2(totals[i]), (ROWS, HDIM))

    attend_own(0, HEADS // 2)

    def send_back(first, count, source_of, target, sent, received):
        def step(peer, carry):
            @pl.when(peer != me)
            def _():
                pltpu.make_async_remote_copy(
                    src_ref=source_of(peer),
                    dst_ref=target,
                    send_sem=sent,
                    recv_sem=received,
                    device_id=(image, peer),
                    device_id_type=MESH,
                ).start()

            @pl.when(peer == me)
            def _():
                pltpu.make_async_copy(source_of(peer), target, received).start()

            return carry

        lax.fori_loop(first, first + count, step, 0)

    @pl.when(is_owner)
    def _():
        for copy in texts:
            copy.wait()
        wait_for(inbox.at[:, keys_queries], kq_sem)
        lane = lax.broadcasted_iota(jnp.int32, (ROWS, HDIM), 1)
        stats = jnp.zeros((ROWS, HDIM), F32)
        k = jnp.concatenate([inbox[:, 0].reshape(BLOCKS * BLK, HDIM), tkeys[...].reshape(TXT, HDIM)], axis=0)
        k = jnp.concatenate([k, kmask[...].reshape(KBLOCKS * BLK, HDIM)], axis=1)
        for chunk in range(CHUNKS):
            peers = slice(chunk * CPEERS, (chunk + 1) * CPEERS)
            blocks = slice(chunk * CBLOCKS, (chunk + 1) * CBLOCKS)
            q = jnp.concatenate(
                [inbox[peers, 1].reshape(CROWS, HDIM), qmask[blocks].reshape(CROWS, HDIM)], axis=1
            )
            scores = nt(q, k)
            top = jnp.max(scores, axis=1, keepdims=True)
            weights = jnp.exp2((scores - top) * SCALE)
            total = jnp.sum(weights, axis=1, keepdims=True)
            pbuf[chunk] = weights.astype(BF16)
            linv[chunk] = jnp.broadcast_to(1.0 / total, (CROWS, HDIM))
            lse = jnp.broadcast_to(top * SCALE + jnp.log2(total), (CROWS, HDIM))
            for i in range(CPEERS):
                stats = jnp.where(lane == chunk * CPEERS + i, lse[i * ROWS : (i + 1) * ROWS], stats)
        turned = jnp.concatenate([stats, jnp.zeros((HDIM - ROWS, HDIM), F32)], axis=0).T
        for peer in range(PEERS):
            lsend[peer] = turned[peer : peer + 1]
        send_back(0, PEERS, lambda peer: lsend.at[peer], lrecv.at[my_head], l_sent, l_sem)

        wait_for(inbox.at[:, only_values], v_sem)
        v = jnp.concatenate([inbox[:, 2].reshape(BLOCKS * BLK, HDIM), tvalues[...].reshape(TXT, HDIM)], axis=0)
        for chunk in range(CHUNKS):
            attended = jnp.dot(pbuf[chunk], v, preferred_element_type=F32) * linv[chunk]
            peers = slice(chunk * CPEERS, (chunk + 1) * CPEERS)
            osend[peers] = attended.astype(BF16).reshape(CPEERS, LIVE, BLK, HDIM)
            send_back(chunk * CPEERS, CPEERS, lambda peer: osend.at[peer], orecv.at[my_head], o_sent, o_sem)

    attend_own(HEADS // 2, HEADS // 2)

    @pl.when(is_owner)
    def _():
        wait_for(inbox.at[pl.ds(0, HEADS - 1), keys_queries], kq_sent)
        wait_for(inbox.at[pl.ds(0, HEADS - 1), only_values], v_sent)

    @pl.when(jnp.logical_not(is_owner))
    def _():
        wait_for(inbox.at[pl.ds(0, HEADS), keys_queries], kq_sent)
        wait_for(inbox.at[pl.ds(0, HEADS), only_values], v_sent)

    wait_for(lrecv, l_sem)
    stacked = jnp.concatenate([lrecv[head] for head in range(HEADS)] + [jnp.zeros((HDIM - HEADS, HDIM), F32)], axis=0)
    columns = stacked.T
    shown = lax.broadcasted_iota(jnp.int32, (LIVE, BLK, HDIM), 0) < n
    for head in range(HEADS):
        sibling = jnp.broadcast_to(columns[:ROWS, head : head + 1], (ROWS, HDIM))
        within = ownlse[head]
        top = jnp.maximum(sibling, within)
        a = jnp.exp2(sibling - top)
        b = jnp.exp2(within - top)
        inverse = 1.0 / (a + b)
        coef[head] = a * inverse
        ownout[head] = ownout[head] * (b * inverse)
    wait_for(orecv, o_sem)
    for head in range(HEADS):
        merged = orecv[head].reshape(ROWS, HDIM).astype(F32) * coef[head] + ownout[head]
        merged = jnp.where(shown, merged.reshape(LIVE, BLK, HDIM), 0.0)
        out[:, :, head * HDIM : (head + 1) * HDIM] = merged.astype(BF16)

    @pl.when(is_owner)
    def _():
        wait_for(lsend.at[pl.ds(0, PEERS - 1)], l_sent)
        wait_for(osend.at[pl.ds(0, PEERS - 1)], o_sent)


def attention(fresh, keys, values, text, slots, lengths):
    anywhere = pl.BlockSpec(memory_space=pl.ANY)
    semaphore = pltpu.SemaphoreType.DMA
    return pl.pallas_call(
        kernel,
        out_shape=jax.ShapeDtypeStruct((LIVE, BLK, HD), BF16),
        in_specs=[anywhere] * 6,
        out_specs=pl.BlockSpec(memory_space=pltpu.VMEM),
        scratch_shapes=[
            pltpu.VMEM((LIVE, BLK, 3 * HD), BF16),
            pltpu.VMEM((2, LIVE, BLK, HD), BF16),
            pltpu.VMEM((HEADS, 3, LIVE, BLK, HDIM), BF16),
            pltpu.VMEM((PEERS, 3, LIVE, BLK, HDIM), BF16),
            pltpu.VMEM((TBLOCKS, BLK, HDIM), BF16),
            pltpu.VMEM((TBLOCKS, BLK, HDIM), BF16),
            pltpu.VMEM((BLOCKS, BLK, HDIM), BF16),
            pltpu.VMEM((KBLOCKS, BLK, HDIM), BF16),
            pltpu.VMEM((CHUNKS, CROWS, KBLOCKS * BLK), BF16),
            pltpu.VMEM((CHUNKS, CROWS, HDIM), F32),
            pltpu.VMEM((PEERS, LIVE, BLK, HDIM), BF16),
            pltpu.VMEM((PEERS, 1, HDIM), F32),
            pltpu.VMEM((HEADS, LIVE, BLK, HDIM), BF16),
            pltpu.VMEM((HEADS, 1, HDIM), F32),
            pltpu.VMEM((HEADS, ROWS, HDIM), F32),
            pltpu.VMEM((HEADS, ROWS, HDIM), F32),
            pltpu.VMEM((HEADS, ROWS, HDIM), F32),
            pltpu.SMEM((2, IMAGES), jnp.int32),
            semaphore((5,)),
            semaphore((2,)),
        ]
        + [semaphore] * 8,
        compiler_params=pltpu.CompilerParams(
            collective_id=0, has_side_effects=True, vmem_limit_bytes=24 * 1024 * 1024
        ),
    )(*[pltpu.with_memory_space_constraint(x, pltpu.HBM) for x in (fresh, keys, values, text, slots, lengths)])


def body(fresh, stale_keys, stale_values, text_kv, group_slots, text_len):
    slot_count = fresh.shape[2]
    text = text_kv[0].reshape(TBLOCKS, BLK, 2 * HD)
    merged = attention(fresh[0, 0], stale_keys[0, 0], stale_values[0, 0], text, group_slots, text_len)
    return jnp.pad(merged, ((0, slot_count - LIVE), (0, 0), (0, 0)))[None, None]


def solution(mesh):
    placed = (
        P("img", "patch", None, None, None),
        P("img", "patch", None, None, None),
        P("img", "patch", None, None, None),
        P("img", None, None),
        P(),
        P(),
    )
    return jax.shard_map(
        body,
        mesh=mesh,
        in_specs=placed,
        out_specs=P("img", "patch", None, None, None),
        check_vma=False,
    )
```

profile of v0, /device:TPU:56, one launch (start us, length us, event | category | flops | bytes accessed | tf_op | source)
XLA Modules:
  0.0 30.3 jit_solution(14379723692256858462)
XLA Ops:
  0.0 29.6 %shard_map.64 = bf16[3,16,1536]{2,1,0:T(8,128)(2,1)S(1)} custom-call(bf16[4,16,4608]{2,1,0:T(8,128)(2,1)} %bitcast.7, bf16[4,16,1536]{2,1,0:T(8,128)(2,1)} %bitcast.8, bf16[4,16,1536]{2,1,0:T(8,128)(2,1)} %bitcast.9, bf16[8,16,3072]{2,1,0:T(8,128)(2,1)} %bitcast.6, s32[32]{0:T(128)} %slots_in.1, s32[32]{0:T(128)} %lengths_in.1), custom_call_target="tpu_custom_call" | custom-call | tf_op jit(solution)/shard_map/pallas_call | solution.py:287
  29.6 0.7 %pad_bitcast_fusion = bf16[1,1,4,16,1536]{4,3,2,1,0:T(8,128)(2,1)} fusion(bf16[3,16,1536]{2,1,0:T(8,128)(2,1)S(1)} %shard_map.64), kind=kLoop, calls=%fused_computation | loop fusion | bytes 344064 | tf_op jit(solution)/shard_map/broadcast_in_dim | solution.py:325
where the time goes:
time: 30.7 us; the launch traced here: 30.3 us
  Pallas kernels  29.6 us (96%)
  local copies, waits for them, and re-layouts  0.69 us (2%)
    pallas_call x1, Pallas kernels, attention(): pl.pallas_call(kernel, out_shape=jax.ShapeDtypeStruct((LIVE, BLK, HD), BF...  29.6 us
    broadcast_in_dim x1, local copies, waits for them, and re-layouts, body(): return jnp.pad(merged, ((0, slot_count - LIVE), (0, 0), (0, 0)))[None, None]  0.69 us

commit v1 on v0

--- a/solution.py
+++ b/solution.py
@@ -54,9 +54,10 @@
 
 def kernel(
     fresh, keys, values, text, slots_in, lengths_in, out,
-    own, stale, chunks, inbox, tkeys, tvalues, qmask, kmask, pbuf, linv,
+    own, stale, chunks, inbox, passing, tkeys, tvalues, qmask, kmask, pbuf, linv,
     osend, lsend, orecv, lrecv, ownout, ownlse, coef, counts,
     local_sem, text_sem, kq_sem, v_sem, o_sem, l_sem, kq_sent, v_sent, o_sent, l_sent,
+    relay_sem, pass_sent,
 ):
     image = lax.axis_index("img")
     me = lax.axis_index("patch")
@@ -110,23 +111,59 @@
     keys_queries = pl.ds(0, 2)
     only_values = pl.ds(2, 1)
 
-    def send(peer, parts, sent, received):
-        pltpu.make_async_remote_copy(
-            src_ref=chunks.at[owned_head(peer, core), parts],
-            dst_ref=inbox.at[me, parts],
+    def remote(source, target, sent, received, peer):
+        return pltpu.make_async_remote_copy(
+            src_ref=source,
+            dst_ref=target,
             send_sem=sent,
             recv_sem=received,
             device_id=(image, peer),
             device_id_type=MESH,
-        ).start()
+        )
+
+    z, x = me // 2, lax.rem(me, 2)
+    opposite = lax.rem(z + 4, 8)
+    downwards = 1 - lax.rem(z, 2)
+    relay = 2 * lax.rem(z + 2 + 4 * downwards, 8) + x
+    origin = lax.rem(z + 6 + 4 * downwards, 8)
+    goal = lax.rem(origin + 4, 8)
+
+    def send_to_relay(parts, which, sent):
+        for side in range(2):
+            peer = 2 * opposite + side
+
+            @pl.when(owner_rank(peer, core) < 3)
+            def _():
+                source = chunks.at[owned_head(peer, core), parts]
+                remote(source, passing.at[side, parts], sent, relay_sem.at[side, which], relay).start()
+
+    def forward(parts, which, received, act):
+        for side in range(2):
+            peer = 2 * goal + side
+
+            @pl.when(owner_rank(peer, core) < 3)
+            def _():
+                held = passing.at[side, parts]
+                act(remote(held, inbox.at[2 * origin + x, parts], pass_sent.at[side, which], received, peer), side)
+
+    def pass_on(parts, which, received):
+        def act(copy, side):
+            held = passing.at[side, parts]
+            pltpu.make_async_copy(held, held, relay_sem.at[side, which]).wait()
+            copy.start()
+
+        forward(parts, which, received, act)
+
+    def passed_on(parts, which, received):
+        forward(parts, which, received, lambda copy, side: copy.wait_send())
 
     def send_all(parts, sent, received):
         def step(k, carry):
             peer = partner(me, k)
 
-            @pl.when(owner_rank(peer, core) < 3)
-            def _():
-                send(peer, parts, sent, received)
+            @pl.when(jnp.logical_and(owner_rank(peer, core) < 3, peer // 2 != opposite))
+            def _():
+                remote(chunks.at[owned_head(peer, core), parts], inbox.at[me, parts], sent, received, peer).start()
 
             return carry
 
@@ -136,8 +173,12 @@
         def _():
             pltpu.make_async_copy(chunks.at[my_head, parts], inbox.at[me, parts], received).start()
 
+    send_to_relay(keys_queries, 0, kq_sent)
+    send_to_relay(only_values, 1, v_sent)
     send_all(keys_queries, kq_sent, kq_sem)
+    pass_on(keys_queries, 0, kq_sem)
     send_all(only_values, v_sent, v_sem)
+    pass_on(only_values, 1, v_sem)
 
     def wait_for(ref, sem):
         pltpu.make_async_copy(ref, ref, sem).wait()
@@ -190,14 +231,7 @@
         def step(peer, carry):
             @pl.when(peer != me)
             def _():
-                pltpu.make_async_remote_copy(
-                    src_ref=source_of(peer),
-                    dst_ref=target,
-                    send_sem=sent,
-                    recv_sem=received,
-                    device_id=(image, peer),
-                    device_id_type=MESH,
-                ).start()
+                remote(source_of(peer), target, sent, received, peer).start()
 
             @pl.when(peer == me)
             def _():
@@ -256,6 +290,9 @@
         wait_for(inbox.at[pl.ds(0, HEADS), keys_queries], kq_sent)
         wait_for(inbox.at[pl.ds(0, HEADS), only_values], v_sent)
 
+    passed_on(keys_queries, 0, kq_sem)
+    passed_on(only_values, 1, v_sem)
+
     wait_for(lrecv, l_sem)
     stacked = jnp.concatenate([lrecv[head] for head in range(HEADS)] + [jnp.zeros((HDIM - HEADS, HDIM), F32)], axis=0)
     columns = stacked.T
@@ -294,6 +331,7 @@
             pltpu.VMEM((2, LIVE, BLK, HD), BF16),
             pltpu.VMEM((HEADS, 3, LIVE, BLK, HDIM), BF16),
             pltpu.VMEM((PEERS, 3, LIVE, BLK, HDIM), BF16),
+            pltpu.VMEM((2, 3, LIVE, BLK, HDIM), BF16),
             pltpu.VMEM((TBLOCKS, BLK, HDIM), BF16),
             pltpu.VMEM((TBLOCKS, BLK, HDIM), BF16),
             pltpu.VMEM((BLOCKS, BLK, HDIM), BF16),
@@ -311,7 +349,8 @@
             semaphore((5,)),
             semaphore((2,)),
         ]
-        + [semaphore] * 8,
+        + [semaphore] * 8
+        + [semaphore((2, 2))] * 2,
         compiler_params=pltpu.CompilerParams(
             collective_id=0, has_side_effects=True, vmem_limit_bytes=24 * 1024 * 1024
         ),

time: 30.7 us -> 30.6 us (level)
  no operation moved by 1% of the time
where the time goes in v1:
time: 30.6 us; the launch traced here: 30.4 us
  Pallas kernels  29.7 us (97%)
  local copies, waits for them, and re-layouts  0.69 us (2%)
    pallas_call x1, Pallas kernels, attention(): pl.pallas_call(kernel, out_shape=jax.ShapeDtypeStruct((LIVE, BLK, HD), BF...  29.7 us
    broadcast_in_dim x1, local copies, waits for them, and re-layouts, body(): return jnp.pad(merged, ((0, slot_count - LIVE), (0, 0), (0, 0)))[None, None]  0.69 us

profile of v1, /device:TPU:56, one launch (start us, length us, event | category | flops | bytes accessed | tf_op | source)
XLA Modules:
  0.0 30.4 jit_solution(14524060870616973291)
XLA Ops:
  0.0 29.7 %shard_map.64 = bf16[3,16,1536]{2,1,0:T(8,128)(2,1)S(1)} custom-call(bf16[4,16,4608]{2,1,0:T(8,128)(2,1)} %bitcast.7, bf16[4,16,1536]{2,1,0:T(8,128)(2,1)} %bitcast.8, bf16[4,16,1536]{2,1,0:T(8,128)(2,1)} %bitcast.9, bf16[8,16,3072]{2,1,0:T(8,128)(2,1)} %bitcast.6, s32[32]{0:T(128)} %slots_in.1, s32[32]{0:T(128)} %lengths_in.1), custom_call_target="tpu_custom_call" | custom-call | tf_op jit(solution)/shard_map/pallas_call | solution.py:324
  29.7 0.7 %pad_bitcast_fusion = bf16[1,1,4,16,1536]{4,3,2,1,0:T(8,128)(2,1)} fusion(bf16[3,16,1536]{2,1,0:T(8,128)(2,1)S(1)} %shard_map.64), kind=kLoop, calls=%fused_computation | loop fusion | bytes 344064 | tf_op jit(solution)/shard_map/broadcast_in_dim | solution.py:364

commit v2 on v0

--- a/solution.py
+++ b/solution.py
@@ -22,11 +22,10 @@
 ROWS = LIVE * BLK
 BLOCKS = PEERS * LIVE
 TBLOCKS = TXT // BLK
-KBLOCKS = BLOCKS + TBLOCKS
-CHUNKS = 4
+KEYS = BLOCKS * BLK + TXT
+CHUNKS = 2
 CPEERS = PEERS // CHUNKS
-CBLOCKS = BLOCKS // CHUNKS
-CROWS = CBLOCKS * BLK
+CROWS = CPEERS * ROWS
 SCALE = 1.4426950408889634 / HDIM**0.5
 MASKED = -1e30
 
@@ -54,7 +53,7 @@
 
 def kernel(
     fresh, keys, values, text, slots_in, lengths_in, out,
-    own, stale, chunks, inbox, tkeys, tvalues, qmask, kmask, pbuf, linv,
+    own, stale, chunks, inbox, tkeys, tvalues, qmask, turned_keys, sbuf, pbuf, linv,
     osend, lsend, orecv, lrecv, ownout, ownlse, coef, counts,
     local_sem, text_sem, kq_sem, v_sem, o_sem, l_sem, kq_sent, v_sent, o_sent, l_sent,
 ):
@@ -149,14 +148,13 @@
 
     @pl.when(is_owner)
     def _():
-        shape = (KBLOCKS, BLK, HDIM)
-        block = lax.broadcasted_iota(jnp.int32, shape, 0)
-        row = lax.broadcasted_iota(jnp.int32, shape, 1)
-        lane = lax.broadcasted_iota(jnp.int32, shape, 2)
+        key = lax.broadcasted_iota(jnp.int32, (1, KEYS), 1)
+        block = (key >> 4) + jnp.where(key < BLOCKS * BLK, 0, HDIM)
         slot = block - 3 * ((block * 171) >> 9)
-        dead = jnp.where(block < BLOCKS, slot - n, (block - BLOCKS) * BLK + row - length) >= 0
-        hit = ((lane == block) & (block < BLOCKS)) | ((lane == HDIM - 1) & dead)
-        kmask[...] = jnp.where(hit, MASKED, 0.0).astype(BF16)
+        past = jnp.where(key < BLOCKS * BLK, slot - n, key - BLOCKS * BLK - length)
+        mark = jnp.where(past >= 0, HDIM - 1, -1)
+        row = lax.broadcasted_iota(jnp.int32, (HDIM, KEYS), 0)
+        turned_keys[HDIM:] = jnp.where((row == block) | (row == mark), MASKED, 0.0).astype(BF16)
         shape = (BLOCKS, BLK, HDIM)
         block = lax.broadcasted_iota(jnp.int32, shape, 0)
         lane = lax.broadcasted_iota(jnp.int32, shape, 2)
@@ -212,25 +210,23 @@
         for copy in texts:
             copy.wait()
         wait_for(inbox.at[:, keys_queries], kq_sem)
+        k = jnp.concatenate([inbox[:, 0].reshape(BLOCKS * BLK, HDIM), tkeys[...].reshape(TXT, HDIM)], axis=0)
+        turned_keys[:HDIM] = k.T
+        q = jnp.concatenate(
+            [inbox[:, 1].reshape(BLOCKS * BLK, HDIM), qmask[...].reshape(BLOCKS * BLK, HDIM)], axis=1
+        )
+        sbuf[...] = jnp.dot(q, turned_keys[...], preferred_element_type=F32)
         lane = lax.broadcasted_iota(jnp.int32, (ROWS, HDIM), 1)
         stats = jnp.zeros((ROWS, HDIM), F32)
-        k = jnp.concatenate([inbox[:, 0].reshape(BLOCKS * BLK, HDIM), tkeys[...].reshape(TXT, HDIM)], axis=0)
-        k = jnp.concatenate([k, kmask[...].reshape(KBLOCKS * BLK, HDIM)], axis=1)
-        for chunk in range(CHUNKS):
-            peers = slice(chunk * CPEERS, (chunk + 1) * CPEERS)
-            blocks = slice(chunk * CBLOCKS, (chunk + 1) * CBLOCKS)
-            q = jnp.concatenate(
-                [inbox[peers, 1].reshape(CROWS, HDIM), qmask[blocks].reshape(CROWS, HDIM)], axis=1
-            )
-            scores = nt(q, k)
+        for peer in range(PEERS):
+            rows = slice(peer * ROWS, (peer + 1) * ROWS)
+            scores = sbuf[rows]
             top = jnp.max(scores, axis=1, keepdims=True)
             weights = jnp.exp2((scores - top) * SCALE)
             total = jnp.sum(weights, axis=1, keepdims=True)
-            pbuf[chunk] = weights.astype(BF16)
-            linv[chunk] = jnp.broadcast_to(1.0 / total, (CROWS, HDIM))
-            lse = jnp.broadcast_to(top * SCALE + jnp.log2(total), (CROWS, HDIM))
-            for i in range(CPEERS):
-                stats = jnp.where(lane == chunk * CPEERS + i, lse[i * ROWS : (i + 1) * ROWS], stats)
+            pbuf[rows] = weights.astype(BF16)
+            linv[rows] = jnp.broadcast_to(1.0 / total, (ROWS, HDIM))
+            stats = jnp.where(lane == peer, top * SCALE + jnp.log2(total), stats)
         turned = jnp.concatenate([stats, jnp.zeros((HDIM - ROWS, HDIM), F32)], axis=0).T
         for peer in range(PEERS):
             lsend[peer] = turned[peer : peer + 1]
@@ -239,7 +235,8 @@
         wait_for(inbox.at[:, only_values], v_sem)
         v = jnp.concatenate([inbox[:, 2].reshape(BLOCKS * BLK, HDIM), tvalues[...].reshape(TXT, HDIM)], axis=0)
         for chunk in range(CHUNKS):
-            attended = jnp.dot(pbuf[chunk], v, preferred_element_type=F32) * linv[chunk]
+            rows = slice(chunk * CROWS, (chunk + 1) * CROWS)
+            attended = jnp.dot(pbuf[rows], v, preferred_element_type=F32) * linv[rows]
             peers = slice(chunk * CPEERS, (chunk + 1) * CPEERS)
             osend[peers] = attended.astype(BF16).reshape(CPEERS, LIVE, BLK, HDIM)
             send_back(chunk * CPEERS, CPEERS, lambda peer: osend.at[peer], orecv.at[my_head], o_sent, o_sem)
@@ -297,9 +294,10 @@
             pltpu.VMEM((TBLOCKS, BLK, HDIM), BF16),
             pltpu.VMEM((TBLOCKS, BLK, HDIM), BF16),
             pltpu.VMEM((BLOCKS, BLK, HDIM), BF16),
-            pltpu.VMEM((KBLOCKS, BLK, HDIM), BF16),
-            pltpu.VMEM((CHUNKS, CROWS, KBLOCKS * BLK), BF16),
-            pltpu.VMEM((CHUNKS, CROWS, HDIM), F32),
+            pltpu.VMEM((2 * HDIM, KEYS), BF16),
+            pltpu.VMEM((BLOCKS * BLK, KEYS), F32),
+            pltpu.VMEM((BLOCKS * BLK, KEYS), BF16),
+            pltpu.VMEM((BLOCKS * BLK, HDIM), F32),
             pltpu.VMEM((PEERS, LIVE, BLK, HDIM), BF16),
             pltpu.VMEM((PEERS, 1, HDIM), F32),
             pltpu.VMEM((HEADS, LIVE, BLK, HDIM), BF16),

time: 30.7 us -> 30.8 us (level)
  Pallas kernels: 29.6 us -> 30 us
    pallas_call x1, Pallas kernels: 29.6 us -> 30 us  [attention(): pl.pallas_call(kernel, out_shape=jax.ShapeDtypeStruct((LIVE, BLK, HD), BF...]
where the time goes in v2:
time: 30.8 us; the launch traced here: 30.7 us
  Pallas kernels  30 us (97%)
  local copies, waits for them, and re-layouts  0.69 us (2%)
    pallas_call x1, Pallas kernels, attention(): pl.pallas_call(kernel, out_shape=jax.ShapeDtypeStruct((LIVE, BLK, HD), BF...  30 us
    broadcast_in_dim x1, local copies, waits for them, and re-layouts, body(): return jnp.pad(merged, ((0, slot_count - LIVE), (0, 0), (0, 0)))[None, None]  0.69 us

profile of v2, /device:TPU:56, one launch (start us, length us, event | category | flops | bytes accessed | tf_op | source)
XLA Modules:
  0.0 30.7 jit_solution(9351414258009985966)
XLA Ops:
  0.0 30.0 %shard_map.64 = bf16[3,16,1536]{2,1,0:T(8,128)(2,1)S(1)} custom-call(bf16[4,16,4608]{2,1,0:T(8,128)(2,1)} %bitcast.7, bf16[4,16,1536]{2,1,0:T(8,128)(2,1)} %bitcast.8, bf16[4,16,1536]{2,1,0:T(8,128)(2,1)} %bitcast.9, bf16[8,16,3072]{2,1,0:T(8,128)(2,1)} %bitcast.6, s32[32]{0:T(128)} %slots_in.1, s32[32]{0:T(128)} %lengths_in.1), custom_call_target="tpu_custom_call" | custom-call | tf_op jit(solution)/shard_map/pallas_call | solution.py:284
  30.0 0.7 %pad_bitcast_fusion = bf16[1,1,4,16,1536]{4,3,2,1,0:T(8,128)(2,1)} fusion(bf16[3,16,1536]{2,1,0:T(8,128)(2,1)S(1)} %shard_map.64), kind=kLoop, calls=%fused_computation | loop fusion | bytes 344064 | tf_op jit(solution)/shard_map/broadcast_in_dim | solution.py:323
